TPU v7x, 128 devices: a whole 4x4x4 slice. The times are simulated.
128 devices in a mesh: wide: 32 (over x_lo, z, y), grp: 4 (over x_hi, core).
Axes of the slice: x: 4 (x_hi: 2, x_lo: 2; x = x_hi * 2 + x_lo), y: 4, z: 4, core: 2. Of those that a mesh axis runs over, the one named last changes fastest.
Arguments:
- tokens: bfloat16 [98304, 768], P(('wide', 'grp')), may hold values from -6 to 6
- exit_layer: int32 [768], P(('wide', 'grp')), may hold values from 1 to 12, as said below
- w_qkv: bfloat16 [768, 2304], P('wide'), may hold values from -0.21875 to 0.21875
- w_out: bfloat16 [768, 768], P('wide'), may hold values from -0.4375 to 0.4375
- gain_attn: bfloat16 [768], P('wide'), may hold values from 0.5 to 1.5
- w_up: bfloat16 [768, 3072], P('wide'), may hold values from -0.21875 to 0.21875
- w_down: bfloat16 [3072, 768], P('wide'), may hold values from -0.109375 to 0.109375
- gain_ffn: bfloat16 [768], P('wide'), may hold values from 0.5 to 1.5
- w_proj: bfloat16 [768, 128], P('wide'), may hold values from -0.21875 to 0.21875
- pool_query: bfloat16 [128], P('wide'), may hold values from -4 to 4
- w_hid: bfloat16 [128, 128], P('wide'), may hold values from -0.5 to 0.5
- w_cls: bfloat16 [128, 14], P('wide'), may hold values from -1 to 1
- cot_out: bfloat16 [98304, 768], P(('wide', 'grp')), may hold values from -6 to 6
- cot_logits: float32 [768, 14], P(('wide', 'grp')), may hold values from -6 to 6
Outputs:
- activations: bfloat16 [98304, 768], P(('wide', 'grp'))
- logits: float32 [768, 14], P(('wide', 'grp'))
- grad_tokens: float32 [98304, 768], P(('wide', 'grp'))
- grad_qkv: float32 [768, 2304], P('wide')
- grad_out: float32 [768, 768], P('wide')
- grad_gain_attn: float32 [768], P('wide')
- grad_up: float32 [768, 3072], P('wide')
- grad_down: float32 [3072, 768], P('wide')
- grad_gain_ffn: float32 [768], P('wide')
- grad_proj: float32 [768, 128], P('wide')
- grad_pool: float32 [128], P('wide')
- grad_hid: float32 [128, 128], P('wide')
- grad_cls: float32 [128, 14], P('wide')
Inputs may be any that keep to these rules, and one draw needn't show every extreme that they name: `exit_layer`: sequences leave early more often than late; some sequence has each end value.
All inputs are finite; a program needn't handle non-finite values.
Results may differ from a plain program's by a relative error of at most 0.033.
Values may be sent and summed in bfloat16 or wider, within the bound.
A program may use at most 192 MiB of HBM per device.

v0:
```python
import jax
import jax.numpy as jnp
from jax import lax
from jax.sharding import PartitionSpec as P

HEADS = 12
HEAD_DIM = 64
SW = 128
POOL_HEADS = 2
SEQ = 128
LAYER = 3


def side_by_side(arrays, axis, dim, along):
    columns = [a.reshape(*a.shape[:along], -1) for a in arrays]
    both = jnp.concatenate(columns, axis=along)
    out, at, outs = (lax.all_gather(both, axis, axis=dim, tiled=True), 0, [])
    for a, column in zip(arrays, columns):
        section = out[..., at : at + column.shape[along]]
        outs.append(section.reshape(*section.shape[:along], *a.shape[along:]))
        at += column.shape[along]
    return tuple(outs)


def split_up(shard, dim, peers):
    shape = shard.shape
    parts = shard.reshape(*shape[:dim], peers, shape[dim] // peers, *shape[dim + 1 :])
    return jnp.moveaxis(parts, dim, 0)


def sum_together(arrays, axis, dims):
    peers = lax.axis_size(axis)
    parts = [split_up(a, dim, peers) for a, dim in zip(arrays, dims)]
    lines = jnp.concatenate([b.reshape(peers, -1) for b in parts], axis=1)
    span = max(16, -(-lines.shape[1] // 1024) * 8)
    lines = jnp.pad(lines, ((0, 0), (0, span * 128 - lines.shape[1]))).reshape(-1, 128)
    line, at, outs = (lax.psum_scatter(lines, axis, tiled=True).reshape(-1), 0, [])
    for b in parts:
        part = b[0]
        outs.append(line[at : at + part.size].reshape(part.shape))
        at += part.size
    return tuple(outs)


def from_everyone(shard, axis):
    peers = lax.axis_size(axis)
    return lax.all_to_all(
        jnp.broadcast_to(shard[None], (peers, *shard.shape)), axis, 0, 0, tiled=True
    )


def over_copies(shard, axis):
    everything = from_everyone(shard, axis)
    return jnp.sum(everything.astype(jnp.float32), axis=0)


def layer_norm(hidden, gain):
    centre = hidden - jnp.mean(hidden, axis=-1, keepdims=True)
    spread = jnp.mean(centre * centre, axis=-1, keepdims=True)
    return centre * lax.rsqrt(spread + 1e-06) * gain


def pool_head(projected, pool_query, w_hid, w_cls):
    seq_count = projected.shape[0] // SEQ
    head_size = SW // POOL_HEADS
    pieces = projected.reshape(seq_count, SEQ, POOL_HEADS, head_size)
    queries = pool_query.reshape(POOL_HEADS, head_size)
    pool_scores = jnp.einsum(
        "bshd,hd->bsh", pieces, queries, precision=lax.Precision.HIGHEST
    ) * head_size ** (-0.5)
    pool_weights = jax.nn.softmax(pool_scores, axis=1)
    pooled = jnp.einsum(
        "bsh,bshd->bhd", pool_weights, pieces, precision=lax.Precision.HIGHEST
    ).reshape(seq_count, SW)
    hidden = jnp.tanh(jnp.dot(pooled, w_hid, precision=lax.Precision.HIGHEST))
    return jnp.dot(hidden, w_cls, precision=lax.Precision.HIGHEST)


def local(
    tokens,
    exit_layer,
    w_qkv,
    w_out,
    gain_attn,
    w_up,
    w_down,
    gain_ffn,
    w_proj,
    pool_query,
    w_hid,
    w_cls,
    cot_out,
    cot_logits,
):
    gathered = (
        *side_by_side((w_qkv, w_out, gain_attn, w_up), "wide", 0, 1),
        lax.all_gather(w_down, "wide", axis=0, tiled=True),
        *side_by_side((gain_ffn, w_proj), "wide", 0, 1),
        *side_by_side((pool_query, w_hid, w_cls), "wide", 0, 1),
    )
    (
        full_qkv,
        full_out,
        full_g1,
        full_up,
        full_down,
        full_g2,
        full_proj,
        full_pool,
        full_hid,
        full_cls,
    ) = gathered
    tok_rows, model_width = tokens.shape
    seq_count = exit_layer.shape[0]
    scale = HEAD_DIM ** (-0.5)
    alive_seq = (exit_layer >= LAYER).astype(jnp.float32)
    alive_tok = jnp.repeat(alive_seq, SEQ)[:, None]
    merged = jnp.dot(tokens, full_qkv, preferred_element_type=jnp.float32).astype(jnp.bfloat16)
    stacked = merged.reshape(seq_count, SEQ, 3, HEADS, HEAD_DIM)
    queries = stacked[:, :, 0]
    key_part = stacked[:, :, 1]
    value_part = stacked[:, :, 2]
    scores = (
        jnp.einsum("bqhd,bkhd->bhqk", queries, key_part, preferred_element_type=jnp.float32) * scale
    )
    top = jnp.max(scores, axis=-1, keepdims=True)
    log_total = top + jnp.log(jnp.sum(jnp.exp(scores - top), axis=-1, keepdims=True))
    probs = jnp.exp(scores - log_total).astype(jnp.bfloat16)
    context = (
        jnp.einsum("bhqk,bkhd->bqhd", probs, value_part, preferred_element_type=jnp.float32)
        .reshape(tok_rows, model_width)
        .astype(jnp.bfloat16)
    )
    mixed = tokens.astype(jnp.float32) + jnp.dot(
        context, full_out, preferred_element_type=jnp.float32
    )
    normed_f, norm1_pull = jax.vjp(layer_norm, mixed, full_g1.astype(jnp.float32))
    normed = normed_f.astype(jnp.bfloat16)
    upward = jnp.dot(normed, full_up, preferred_element_type=jnp.float32)
    active_f, gelu_pull = jax.vjp(jax.nn.gelu, upward)
    active = active_f.astype(jnp.bfloat16)
    second = normed.astype(jnp.float32) + jnp.dot(
        active, full_down, preferred_element_type=jnp.float32
    )
    output_f, norm2_pull = jax.vjp(layer_norm, second, full_g2.astype(jnp.float32))
    output = output_f.astype(jnp.bfloat16)
    projected = jnp.dot(output, full_proj, preferred_element_type=jnp.float32)
    student_out, head_pull = jax.vjp(
        pool_head,
        projected,
        full_pool.astype(jnp.float32),
        full_hid.astype(jnp.float32),
        full_cls.astype(jnp.float32),
    )
    activations = (output.astype(jnp.float32) * alive_tok).astype(jnp.bfloat16)
    logits = student_out * alive_seq[:, None]
    grad_projected, grad_pool, grad_hid, grad_cls = head_pull(cot_logits * alive_seq[:, None])
    proj_low = grad_projected.astype(jnp.bfloat16)
    grad_proj = jnp.einsum("nd,ns->ds", output, proj_low, preferred_element_type=jnp.float32)
    grad_output = cot_out.astype(jnp.float32) * alive_tok + jnp.einsum(
        "ns,ds->nd", proj_low, full_proj, preferred_element_type=jnp.float32
    )
    grad_second, grad_g2 = norm2_pull(grad_output)
    down_low = grad_second.astype(jnp.bfloat16)
    grad_down = jnp.einsum("nf,nd->fd", active, down_low, preferred_element_type=jnp.float32)
    grad_active = jnp.einsum("nd,fd->nf", down_low, full_down, preferred_element_type=jnp.float32)
    (grad_upward,) = gelu_pull(grad_active)
    up_low = grad_upward.astype(jnp.bfloat16)
    grad_up = jnp.einsum("nd,nf->df", normed, up_low, preferred_element_type=jnp.float32)
    grad_normed = grad_second + jnp.einsum(
        "nf,df->nd", up_low, full_up, preferred_element_type=jnp.float32
    )
    grad_mixed, grad_g1 = norm1_pull(grad_normed)
    attn_low = grad_mixed.astype(jnp.bfloat16)
    grad_out = jnp.einsum("ni,nd->id", context, attn_low, preferred_element_type=jnp.float32)
    context_low = jnp.einsum(
        "nd,id->ni", attn_low, full_out, preferred_element_type=jnp.float32
    ).astype(jnp.bfloat16)
    context_low = context_low.reshape(seq_count, SEQ, HEADS, HEAD_DIM)
    probs_f = jnp.exp(
        jnp.einsum("bqhd,bkhd->bhqk", queries, key_part, preferred_element_type=jnp.float32) * scale
        - log_total
    )
    probs_low = probs_f.astype(jnp.bfloat16)
    grad_probs = jnp.einsum(
        "bqhd,bkhd->bhqk", context_low, value_part, preferred_element_type=jnp.float32
    )
    grad_values = jnp.einsum(
        "bhqk,bqhd->bkhd", probs_low, context_low, preferred_element_type=jnp.float32
    )
    grad_scores = probs_f * (grad_probs - jnp.sum(probs_f * grad_probs, axis=-1, keepdims=True))
    scores_low = grad_scores.astype(jnp.bfloat16)
    grad_queries = (
        jnp.einsum("bhqk,bkhd->bqhd", scores_low, key_part, preferred_element_type=jnp.float32)
        * scale
    )
    grad_keys = (
        jnp.einsum("bhqk,bqhd->bkhd", scores_low, queries, preferred_element_type=jnp.float32)
        * scale
    )
    merged_low = (
        jnp.stack([grad_queries, grad_keys, grad_values], axis=2)
        .reshape(tok_rows, 3 * model_width)
        .astype(jnp.bfloat16)
    )
    grad_qkv = jnp.einsum("nd,nc->dc", tokens, merged_low, preferred_element_type=jnp.float32)
    grad_tokens = grad_mixed + jnp.einsum(
        "nc,dc->nd", merged_low, full_qkv, preferred_element_type=jnp.float32
    )
    shards = tuple(
        (
            part.astype(jnp.float32)
            for part in sum_together(
                (
                    grad_qkv.astype(jnp.bfloat16),
                    grad_out.astype(jnp.bfloat16),
                    grad_g1.astype(jnp.bfloat16),
                    grad_up.astype(jnp.bfloat16),
                    grad_down.astype(jnp.bfloat16),
                    grad_g2.astype(jnp.bfloat16),
                    grad_proj.astype(jnp.bfloat16),
                    grad_pool.astype(jnp.bfloat16),
                    grad_hid.astype(jnp.bfloat16),
                    grad_cls.astype(jnp.bfloat16),
                ),
                "wide",
                (0, 0, 0, 0, 0, 0, 0, 0, 0, 0),
            )
        )
    )
    summed = (
        over_copies(shards[0].astype(jnp.bfloat16), "grp").astype(jnp.float32),
        over_copies(shards[1].astype(jnp.bfloat16), "grp").astype(jnp.float32),
        over_copies(shards[2].astype(jnp.bfloat16), "grp").astype(jnp.float32),
        over_copies(shards[3].astype(jnp.bfloat16), "grp").astype(jnp.float32),
        over_copies(shards[4].astype(jnp.bfloat16), "grp").astype(jnp.float32),
        over_copies(shards[5].astype(jnp.bfloat16), "grp").astype(jnp.float32),
        over_copies(shards[6].astype(jnp.bfloat16), "grp").astype(jnp.float32),
        over_copies(shards[7].astype(jnp.bfloat16), "grp").astype(jnp.float32),
        over_copies(shards[8].astype(jnp.bfloat16), "grp").astype(jnp.float32),
        over_copies(shards[9].astype(jnp.bfloat16), "grp").astype(jnp.float32),
    )
    return (
        activations,
        logits,
        grad_tokens,
        summed[0],
        summed[1],
        summed[2],
        summed[3],
        summed[4],
        summed[5],
        summed[6],
        summed[7],
        summed[8],
        summed[9],
    )


def solution(mesh):
    in_specs = (
        P(("wide", "grp"), None),
        P(("wide", "grp")),
        P("wide", None),
        P("wide", None),
        P("wide"),
        P("wide", None),
        P("wide", None),
        P("wide"),
        P("wide", None),
        P("wide"),
        P("wide", None),
        P("wide", None),
        P(("wide", "grp"), None),
        P(("wide", "grp"), None),
    )
    out_specs = (
        P(("wide", "grp"), None),
        P(("wide", "grp"), None),
        P(("wide", "grp"), None),
        P("wide", None),
        P("wide", None),
        P("wide"),
        P("wide", None),
        P("wide", None),
        P("wide"),
        P("wide", None),
        P("wide"),
        P("wide", None),
        P("wide", None),
    )
    return jax.shard_map(local, mesh=mesh, in_specs=in_specs, out_specs=out_specs, check_vma=False)
```

profile of v0, /device:TPU:1, one launch (start us, length us, event | category | flops | bytes accessed | tf_op | source)
XLA Modules:
  0.0 906.2 jit_solution(4984616593483814877)
XLA Ops:
  8.1 1.9 concatenate.12
  12.3 73.6 %all-gather = bf16[32,4,143]{2,1,0:T(4,128)(2,1)S(1)} all-gather(bf16[1,4,143]{2,1,0:T(4,128)(2,1)S(1)} %maximum_bitcast_fusion), channel_id=1, replica_groups=mesh['wide'=32,'grp'=4] {'wide'}, dimensions={0}, use_global_device_ids=true | all-gather | bytes 37752 | tf_op jit(solution)/shard_map/all_gather | solution.py:17
  88.1 2.4 copy.180
  92.1 68.8 %all_gather.14 = bf16[768,129]{1,0:T(8,128)(2,1)S(1)} all-gather(bf16[24,129]{1,0:T(8,128)(2,1)S(1)} %pad_maximum_fusion.1), channel_id=1, replica_groups=mesh['wide'=32,'grp'=4] {'wide'}, dimensions={0}, use_global_device_ids=true | all-gather | bytes 204336 | tf_op jit(solution)/shard_map/all_gather | solution.py:17
  161.9 5.4 all-gather.4.cloned.1.call-done
  167.3 5.3 fusion.7
  172.6 5.6 reshape.218
  178.2 3.3 fusion.90
  184.4 1.7 copy-done
  192.0 6.7 fusion.11
  198.6 128.2 %all-gather.6.cloned.1.call-done = bf16[3072,768]{1,0:T(8,128)(2,1)} async-done(((bf16[96,768]{1,0:T(8,128)(2,1)}), bf16[3072,768]{1,0:T(8,128)(2,1)}) %all-gather.6.cloned.1.call-update) | async-done | bytes 4718608 | tf_op jit(solution)/shard_map/all_gather | solution.py:97
  326.8 9.8 %fusion.94 = (f32[768]{0:T(1024)S(1)}, f32[768,768]{0,1:T(8,128)S(1)}) fusion(bf16[3072,768]{1,0:T(8,128)(2,1)} %all-gather.6.cloned.1.call-done, f32[768,3072]{1,0:T(8,128)} %fusion.11, bf16[768,768]{0,1:T(8,128)(2,1)S(1)} %multiply_convert_fusion.6), kind=kOutput, calls=%fused_computation.170 | convolution fusion | flops 3646881024 | bytes 17697792 | tf_op jit(solution)/shard_map/dot_general | solution.py:142
  340.3 1.9 reshape.222
  345.0 2.4 fusion.45
  350.8 1.6 convolution_convert_fusion.10
  352.4 1.7 fusion.60
  358.5 1.6 fusion.43
  364.1 1.7 multiply_reduce_fusion.2
  367.8 10.6 %convolution_convert_fusion.2 = bf16[3072,768]{1,0:T(8,128)(2,1)} fusion(f32[768,768]{0,1:T(8,128)S(1)} %get-tuple-element.111, f32[768]{0:T(1024)S(1)} %negate_multiply_fusion.1, f32[768,3072]{1,0:T(8,128)} %fusion.11), kind=kOutput, calls=%fused_computation.12 | convolution fusion | flops 3648651264 | bytes 16518144 | tf_op jit(solution)/shard_map/nf,nd->fd/dot_general | solution.py:165
  378.4 14.0 %fusion.6 = bf16[768,3072]{1,0:T(8,128)(2,1)} fusion(f32[768,3072]{1,0:T(8,128)S(1)} %bitcast.196, bf16[3072,768]{1,0:T(8,128)(2,1)} %all-gather.6.cloned.1.call-done, f32[768,768]{0,1:T(8,128)} %copy-done.22, f32[768]{0:T(1024)S(1)} %negate_multiply_fusion.1), kind=kOutput, calls=%fused_computation.8 | convolution fusion | flops 3672244224 | bytes 21236736 | tf_op jit(solution)/shard_map/nd,fd->nf/dot_general | solution.py:166
  392.5 8.0 convolution_convert_fusion.3
  400.6 4.8 multiply_reduce_fusion.3
  406.8 2.2 convolution_convert_fusion.4
  409.0 2.2 convolution_convert_fusion.6
  411.2 3.4 reshape.243
  414.6 3.0 copy.183
  417.6 4.6 fusion.28
  422.2 3.8 multiply_reduce_fusion
  427.5 1.7 fusion.30
  434.4 1.7 reshape_reshape.25
  436.1 6.0 reshape_reshape.24
  442.1 6.1 reshape_reshape.23
  448.3 2.4 reshape_reshape.22
  452.6 3.3 copy.188
  456.0 2.1 copy-done.13
  458.1 4.7 fusion.8
  462.7 4.3 copy.190
  467.0 3.2 reshape_reshape.21
  470.2 4.2 constant_dynamic-update-slice_fusion.1
  476.8 27.5 %dynamic-update-slice.3 = bf16[32,224876]{1,0:T(8,128)(2,1)} dynamic-update-slice(bf16[32,224876]{1,0:T(8,128)(2,1)} %dynamic-update-slice.2, bf16[32,73728]{1,0:T(8,128)(2,1)} %reshape_reshape.23, s32[]{} %constant.59, s32[]{} %constant.62) | dynamic-update-slice | bytes 9437188
  504.4 27.5 %dynamic-update-slice.4 = bf16[32,224876]{1,0:T(8,128)(2,1)} dynamic-update-slice(bf16[32,224876]{1,0:T(8,128)(2,1)} %dynamic-update-slice.3, bf16[32,73728]{1,0:T(8,128)(2,1)} %reshape_reshape.24, s32[]{} %constant.59, s32[]{} %constant.63) | dynamic-update-slice | bytes 9437188
  533.3 3.4 dynamic-update-slice.6
  538.3 1.6 dynamic-update-slice.8
  541.2 14.0 %pad.4 = bf16[32,225280]{1,0:T(8,128)(2,1)} pad(bf16[32,224876]{1,0:T(8,128)(2,1)} %dynamic-update-slice.9, bf16[]{:T(256)} %constant.41.clone.1), padding=0_0x0_404 | pad | bytes 28809986 | tf_op jit(solution)/shard_map/jit(_pad)/pad | solution.py:36
  555.2 13.3 %reshape.226 = bf16[56320,128]{1,0:T(8,128)(2,1)} reshape(bf16[32,225280]{1,0:T(8,128)(2,1)} %pad.4) | data formatting | bytes 28835840 | tf_op jit(solution)/shard_map/reshape | solution.py:36
  568.6 193.3 %reduce-scatter.2.cloned.1.call-done = bf16[1760,128]{1,0:T(8,128)(2,1)} async-done(((bf16[56320,128]{1,0:T(8,128)(2,1)}), bf16[1760,128]{1,0:T(8,128)(2,1)}) %reduce-scatter.2.cloned.1.call-update) | async-done | bytes 450576 | tf_op jit(solution)/shard_map/reduce_scatter | solution.py:37
  763.3 28.2 %all_to_all.53 = bf16[4,1,4]{2,1,0:T(2,128)(2,1)} all-to-all(bf16[4,1,4]{2,1,0:T(2,128)(2,1)S(1)} %broadcast_in_dim.123), channel_id=1, replica_groups=mesh['wide'=32,'grp'=4] {'grp'}, dimensions={0} | all-to-all | bytes 64 | tf_op jit(solution)/shard_map/all_to_all | solution.py:47
  791.5 7.7 all_to_all.54
  799.9 3.9 all-to-all-start.5
  804.6 3.6 all-to-all-done.5
  808.8 3.9 all-to-all-start.9
  813.5 3.8 all-to-all-done.9
  817.9 3.9 all-to-all-start.8
  822.6 3.8 all-to-all-done.8
  827.1 4.5 all-to-all-start.6
  831.6 7.8 add_add_fusion.2
  843.8 4.8 all-to-all-start.1
  851.7 1.9 copy.196
  854.8 4.6 all-to-all-start
  860.3 7.7 all-to-all-done
  868.8 4.3 all-to-all-start.3
  875.4 7.9 all-to-all-done.3
  884.2 4.3 all-to-all-start.4
  893.0 5.7 all-to-all-done.4
  (263 shorter events, 78.4 us)
Async XLA Ops:
  7.2 83.4 %copy-start.29 = (bf16[768,768]{1,0:T(8,128)(2,1)S(1)}, bf16[768,768]{1,0:T(8,128)(2,1)}, u32[]{:S(2)}) copy-start(bf16[768,768]{1,0:T(8,128)(2,1)} %param.14) | copy-start | bytes 3538948
  7.2 160.1 %all-gather.4.cloned.1.call-start = ((), (), s32[]{:S(2)}) async-start(), calls=%async_computation.11 | async-start | bytes 9934848 | tf_op jit(solution)/shard_map/all_gather | solution.py:17
  10.0 316.9 %all-gather.6.cloned.1.call-start = ((), (), s32[]{:S(2)}) async-start(), calls=%async_computation.12 | async-start | bytes 4866048 | tf_op jit(solution)/shard_map/all_gather | solution.py:97
  10.7 751.1 %reduce-scatter.2.cloned.1.call-start = ((), (), s32[]{:S(2)}) async-start(), calls=%async_computation.13 | async-start | bytes 14868480 | tf_op jit(solution)/shard_map/reduce_scatter | solution.py:37
  86.0 6.0 copy-start.34
  88.1 3.9 copy-start.57
  88.1 73.7 %copy-start.62 = (s32[6]{0:T(128)S(1)}, s32[6]{0:T(128)}, u32[]{:S(2)}) copy-start(s32[6]{0:T(128)} %param.15) | copy-start | bytes 76
  161.8 10.8 %copy-start.61 = (f32[6]{0:T(128)}, f32[6]{0:T(128)S(1)}, u32[]{:S(2)}) copy-start(f32[6]{0:T(128)S(1)} %compare_convert_fusion) | copy-start | bytes 76
  161.9 175.7 %copy-start.42 = (f32[768]{0:T(1024)}, f32[768]{0:T(1024)S(1)}, u32[]{:S(2)}) copy-start(f32[768]{0:T(1024)S(1)} %broadcast_bitcast_fusion) | copy-start | bytes 9220
  178.2 9.8 %slice-start.5 = ((s8[9633792]{0:T(1024)(128)(4,1)}), s8[1245184]{0:T(1024)(128)(4,1)S(1)}, s32[]{:S(2)}) async-start(s8[9633792]{0:T(1024)(128)(4,1)} %bitcast.199), calls=%async_computation.19 | async-start | bytes 2490368
  181.5 2.9 copy-start.4
  181.5 6.5 slice-start.6
  183.2 3.0 copy-start
  183.2 5.1 slice-start.7
  188.4 1.9 copy-start.48
  190.3 8.3 copy-start.44
  192.0 134.9 %copy-start.15 = (bf16[768,768]{0,1:T(8,128)(2,1)}, bf16[768,768]{0,1:T(8,128)(2,1)S(1)}, u32[]{:S(2)}) copy-start(bf16[768,768]{0,1:T(8,128)(2,1)S(1)} %multiply_convert_fusion.6) | copy-start | bytes 3538948
  343.7 3.7 copy-start.55
  358.5 5.6 copy-start.11
  358.5 5.6 copy-start.19
  358.5 5.6 copy-start.37
  358.5 5.6 copy-start.43
  361.7 4.1 copy-start.40
  365.8 12.6 %slice-start.2 = ((s8[9437184]{0:T(1024)(128)(4,1)}), s8[4194304]{0:T(1024)(128)(4,1)S(1)}, s32[]{:S(2)}) async-start(s8[9437184]{0:T(1024)(128)(4,1)} %bitcast.195), calls=%async_computation.16 | async-start | bytes 8388608
  367.8 10.6 %slice-start.3 = ((s8[9437184]{0:T(1024)(128)(4,1)}), s8[4194304]{0:T(1024)(128)(4,1)S(1)}, s32[]{:S(2)}) async-start(s8[9437184]{0:T(1024)(128)(4,1)} %bitcast.195), calls=%async_computation.17 | async-start | bytes 8388608
  367.8 10.6 %slice-start.4 = ((s8[9437184]{0:T(1024)(128)(4,1)}), s8[1048576]{0:T(1024)(128)(4,1)S(1)}, s32[]{:S(2)}) async-start(s8[9437184]{0:T(1024)(128)(4,1)} %bitcast.195), calls=%async_computation.18 | async-start | bytes 2097152
  367.8 32.7 %slice-start.8 = ((s8[9633792]{0:T(1024)(128)(4,1)}), s8[4194304]{0:T(1024)(128)(4,1)S(1)}, s32[]{:S(2)}) async-start(s8[9633792]{0:T(1024)(128)(4,1)} %bitcast.201), calls=%async_computation.22 | async-start | bytes 8388608
  378.4 14.1 %copy-start.16 = (bf16[768,768]{0,1:T(8,128)(2,1)S(1)}, bf16[768,768]{0,1:T(8,128)(2,1)}, u32[]{:S(2)}) copy-start(bf16[768,768]{0,1:T(8,128)(2,1)} %copy-done.15) | copy-start | bytes 3538948
  378.4 22.1 %slice-start.9 = ((s8[9633792]{0:T(1024)(128)(4,1)}), s8[4194304]{0:T(1024)(128)(4,1)S(1)}, s32[]{:S(2)}) async-start(s8[9633792]{0:T(1024)(128)(4,1)} %bitcast.201), calls=%async_computation.23 | async-start | bytes 8388608
  378.4 22.1 %slice-start.10 = ((s8[9633792]{0:T(1024)(128)(4,1)}), s8[1245184]{0:T(1024)(128)(4,1)S(1)}, s32[]{:S(2)}) async-start(s8[9633792]{0:T(1024)(128)(4,1)} %bitcast.201), calls=%async_computation.24 | async-start | bytes 2490368
  392.5 8.1 copy-start.2
  392.5 8.1 copy-start.23
  392.5 8.1 copy-start.39
  392.5 8.1 copy-start.49
  392.5 8.1 copy-start.51
  392.5 8.1 copy-start.63
  400.6 4.8 copy-start.45
  406.0 3.0 copy-start.20
  406.0 2.9 copy-start.60
  414.6 3.0 copy-start.28
  417.6 4.6 copy-start.3
  417.6 4.6 copy-start.5
  417.6 8.4 slice-start
  422.2 3.8 slice-start.1
  429.2 3.6 copy-start.59
  452.6 5.5 copy-start.30
  456.0 2.1 copy-start.13
  470.2 4.2 copy-start.12
  504.4 29.0 %copy-start.32 = (bf16[32,3072]{1,0:T(8,128)(2,1)S(1)}, bf16[32,3072]{1,0:T(8,128)(2,1)}, u32[]{:S(2)}) copy-start(bf16[32,3072]{1,0:T(8,128)(2,1)} %reshape_reshape.25) | copy-start | bytes 589828
  504.4 32.4 %copy-start.53 = (bf16[32,4]{1,0:T(8,128)(2,1)S(1)}, bf16[32,4]{1,0:T(8,128)(2,1)}, u32[]{:S(2)}) copy-start(bf16[32,4]{1,0:T(8,128)(2,1)} %convert_element_type.232) | copy-start | bytes 772
  504.4 33.9 %copy-start.35 = (bf16[32,512]{1,0:T(8,128)(2,1)S(1)}, bf16[32,512]{1,0:T(8,128)(2,1)}, u32[]{:S(2)}) copy-start(bf16[32,512]{1,0:T(8,128)(2,1)} %reshape_reshape.26) | copy-start | bytes 98308
  568.5 263.0 %copy-start.21 = (f32[768,768]{0,1:T(8,128)S(1)}, f32[768,768]{0,1:T(8,128)}, u32[]{:S(2)}) copy-start(f32[768,768]{0,1:T(8,128)} %copy-done.20) | copy-start | bytes 7077892
  799.9 8.4 all-to-all-start.5
  808.8 8.5 all-to-all-start.9
  817.9 8.5 all-to-all-start.8
  827.1 15.3 %all-to-all-start.6 = ((bf16[4,24,128]{2,1,0:T(8,128)(2,1)}), bf16[4,24,128]{2,1,0:T(8,128)(2,1)}, u32[]{:S(2)}, u32[]{:S(2)}) async-start(bf16[4,24,128]{2,1,0:T(8,128)(2,1)} %broadcast_in_dim.122), calls=%async_computation.7 | async-start | bytes 49152 | tf_op jit(solution)/shard_map/all_to_all | solution.py:47
  831.6 18.6 %copy-start.14 = (bf16[768,768]{0,1:T(8,128)(2,1)S(1)}, bf16[768,768]{0,1:T(8,128)(2,1)}, u32[]{:S(2)}) copy-start(bf16[768,768]{0,1:T(8,128)(2,1)} %get-tuple-element.112) | copy-start | bytes 3538948
  839.4 12.2 %copy-start.24 = (f32[768,768]{0,1:T(8,128)S(1)}, f32[768,768]{0,1:T(8,128)}, u32[]{:S(2)}) copy-start(f32[768,768]{0,1:T(8,128)} %add_add_fusion.2) | copy-start | bytes 7077892
  843.8 10.1 %all-to-all-start.1 = ((bf16[4,24,768]{2,1,0:T(8,128)(2,1)}), bf16[4,24,768]{2,1,0:T(8,128)(2,1)}, u32[]{:S(2)}, u32[]{:S(2)}) async-start(bf16[4,24,768]{2,1,0:T(8,128)(2,1)} %broadcast_in_dim.55), calls=%async_computation.2 | async-start | bytes 294912 | tf_op jit(solution)/shard_map/all_to_all | solution.py:47
  851.6 1.9 copy-start.33
  853.6 6.2 copy-start.56
  854.8 13.2 %all-to-all-start = ((bf16[4,24,2304]{2,1,0:T(8,128)(2,1)}), bf16[4,24,2304]{2,1,0:T(8,128)(2,1)S(1)}, u32[]{:S(2)}, u32[]{:S(2)}) async-start(bf16[4,24,2304]{2,1,0:T(8,128)(2,1)} %broadcast_in_dim.53), calls=%async_computation.1 | async-start | bytes 884736 | tf_op jit(solution)/shard_map/all_to_all | solution.py:47
  868.8 14.5 %all-to-all-start.3 = ((bf16[4,24,3072]{2,1,0:T(8,128)(2,1)}), bf16[4,24,3072]{2,1,0:T(8,128)(2,1)S(1)}, u32[]{:S(2)}, u32[]{:S(2)}) async-start(bf16[4,24,3072]{2,1,0:T(8,128)(2,1)} %broadcast_in_dim.58), calls=%async_computation.4 | async-start | bytes 1179648 | tf_op jit(solution)/shard_map/all_to_all | solution.py:47
  884.2 14.5 %all-to-all-start.4 = ((bf16[4,96,768]{2,1,0:T(8,128)(2,1)}), bf16[4,96,768]{2,1,0:T(8,128)(2,1)S(1)}, u32[]{:S(2)}, u32[]{:S(2)}) async-start(bf16[4,96,768]{2,1,0:T(8,128)(2,1)} %broadcast_in_dim.119), calls=%async_computation.5 | async-start | bytes 1179648 | tf_op jit(solution)/shard_map/all_to_all | solution.py:47
  (22 other events, 28.5 us)
Sparse Core Ops, SparseCore 0:
  10.2 157.0 all-gather.3
  169.0 157.8 all-gather.5
  568.7 193.0 reduce-scatter.1
where the time goes:
time: 915 us; the launch traced here: 906 us
  waiting for transfers between devices  360 us (39%)
  local copies, waits for them, and re-layouts  189 us (21%)
  blocking collectives  178 us (19%)
  matrix products  108 us (12%)
  starting transfers between devices  34.4 us (4%)
  other arithmetic  20.7 us (2%)
  between operations  14.9 us (2%)
    reduce_scatter x1, waiting for transfers between devices, sum_together(): lax.psum_scatter(lines, axis, tiled=True).reshape(-1)  193 us
    all_gather x2, blocking collectives, side_by_side(): out, at, outs = (lax.all_gather(both, axis, axis=dim, tiled=True), 0, [])  142 us
    all_gather x1, waiting for transfers between devices, local(): lax.all_gather(w_down, 'wide', axis=0, tiled=True)  128 us
    unnamed x164, local copies, waits for them, and re-layouts  87.3 us
    all_to_all x2, blocking collectives, from_everyone(): lax.all_to_all(jnp.broadcast_to(shard[None], (peers, *shard.shape)), axis...  35.9 us
    all_to_all x8, starting transfers between devices, from_everyone(): lax.all_to_all(jnp.broadcast_to(shard[None], (peers, *shard.shape)), axis...  34.3 us
    all_to_all x8, waiting for transfers between devices, from_everyone(): lax.all_to_all(jnp.broadcast_to(shard[None], (peers, *shard.shape)), axis...  32.9 us
    another operation x7, local copies, waits for them, and re-layouts, sum_together(): lines = jnp.concatenate([b.reshape(peers, -1) for b in parts], axis=1)  21.7 us
  transfers between devices with their start and end apart: 11, of which 10 were waited for; matrix products, arithmetic and copies ran while one was open for 7% of the time, Pallas kernels for 0%

commit v1 on v0

v1 whole, which is shorter than its diff:
```python
import functools
import jax
import jax.numpy as jnp
from jax import lax
from jax.sharding import PartitionSpec as P
from jax.experimental import pallas as pl
from jax.experimental.pallas import tpu as pltpu

D = 768
FF = 3072
TOK = 768
SEQ_DEV = 6
PAIRS = 6
SEQ = 128
LAYER = 3
MESH = pl.DeviceIdType.MESH
BF = jnp.bfloat16
F32 = jnp.float32
SIZE = {"x": 2, "z": 4, "y": 4}
ORDERS = (
    (("y", "z", "x"), ("z", "x", "y"), ("y", "x", "z")),
    (("z", "y", "x"), ("z", "x", "y"), ("y", "x", "z")),
)
EVENTS = 7
SUMS = 8
VMEM = 62 * 2**20


class Place:
    def __init__(self):
        wide, grp = lax.axis_index("wide"), lax.axis_index("grp")
        xl, z, y = wide // 16, (wide // 4) % 4, wide % 4
        x = (grp // 2) * 2 + xl
        self.core = grp % 2
        self.places = {("x", 0): xl, ("x", 1): 1 - xl}
        for axis, here in (("z", z), ("y", y)):
            for step in range(4):
                self.places[axis, step] = (here + step) % 4
        self.ids = {}
        for step in (1, 2, 3):
            far = (x + step) % 4
            self.ids["x", step] = ((far % 2) * 16 + z * 4 + y, (far // 2) * 2 + self.core)
            self.ids["y", step] = (xl * 16 + z * 4 + self.places["y", step], grp)
            self.ids["z", step] = (xl * 16 + self.places["z", step] * 4 + y, grp)
        self.sibling = (wide, grp + 1 - 2 * self.core)

    def near(self, axis, step):
        return self.ids[axis, step % 4]

    def at(self, axis, step=0):
        return self.places[axis, step % SIZE[axis]]

    def box(self, have, **fixed):
        out = []
        for axis in ("x", "z", "y"):
            if axis in fixed:
                out.append(fixed[axis])
            elif axis in have:
                out.append(slice(None))
            else:
                out.append(self.at(axis))
        return tuple(out)

    def on_core(self, step):
        for core in (0, 1):
            pl.when(self.core == core)(functools.partial(step, core))


def greet(place):
    barrier = pltpu.get_barrier_semaphore()
    ids = [place.near(a, s) for a in ("x", "y", "z") for s in (1, -1)] + [place.near("x", 2), place.sibling]
    for i in ids:
        pl.semaphore_signal(barrier, inc=1, device_id=i, device_id_type=MESH)
    pl.semaphore_wait(barrier, len(ids))


class Wire:
    def __init__(self, send, recv):
        self.send, self.recv = send, recv
        self.started = []

    def copy(self, n, src, dst, to):
        return pltpu.make_async_remote_copy(
            src_ref=src, dst_ref=dst, send_sem=self.send.at[n], recv_sem=self.recv.at[n],
            device_id=to, device_id_type=MESH,
        )

    def go(self, n, src, dst, to):
        self.copy(n, src, dst, to).start()
        self.started.append((n, src, dst, to))

    def landed(self, n, dst, to):
        self.copy(n, dst, dst, to).wait_recv()

    def sent(self):
        for c in self.started:
            self.copy(*c).wait_send()


def piece(kind, core, k, width):
    if kind == "cols":
        return (slice(None), pl.ds((core * 3 + k) * (width // 6), width // 6))
    return (pl.ds(core * 16, 16), slice(None)) if k == 1 else None


def gather_unit(place, wire, base, sib, core, order, own, full):
    way = 1 if core == 0 else -1
    have, e = [], 0
    for axis in order:
        mine = place.box(have)
        src = full(mine) if have else own
        ahead, back = place.near(axis, way), place.near(axis, -way)
        if axis == "x":
            wire.go(base + e, src, full(mine), ahead)
            yield
            got = place.box(have, x=place.at("x", 1))
            wire.landed(base + e, full(got), ahead)
            sib(e, got)
            e += 1
        else:
            wire.go(base + e, src, full(mine), ahead)
            wire.go(base + e + 1, src, full(mine), back)
            yield
            got = place.box(have, **{axis: place.at(axis, -way)})
            wire.landed(base + e, full(got), ahead)
            wire.go(base + e + 2, full(got), full(got), ahead)
            sib(e, got)
            yield
            for late, step in ((1, way), (2, 2)):
                got = place.box(have, **{axis: place.at(axis, step)})
                wire.landed(base + e + late, full(got), ahead)
                sib(e + late, got)
            e += 3
        have.append(axis)


def passed_on(place, core, order):
    way = 1 if core == 0 else -1
    have, out = [], []
    for axis in order:
        if axis == "x":
            out.append(place.box(have, x=place.at("x", 1)))
        else:
            out.extend(place.box(have, **{axis: place.at(axis, s)}) for s in (-way, way, 2))
        have.append(axis)
    return out


class Gather:
    def __init__(self, place, kinds, shards, fulls, send, recv, ssend, srecv, lsem):
        self.place, self.kinds, self.shards, self.fulls = place, kinds, shards, fulls
        self.wires = [Wire(send, recv) for _ in range(2)]
        self.sides = [Wire(ssend, srecv) for _ in range(2)]
        self.keep = Wire(lsem, lsem)
        n = len(kinds)
        self.units = [[[] for _ in range(n)] for _ in range(2)]
        for core in range(2):
            for i in range(n):
                for k in range(3):
                    tail = self.tail(core, i, k)
                    if tail is None:
                        continue
                    full = functools.partial(self.part, i, tail)
                    sib = functools.partial(self.pass_on, core, i, k, full)
                    self.units[core][i].append(gather_unit(
                        place, self.wires[core], (i * 3 + k) * EVENTS, sib, core, ORDERS[core][k],
                        shards[i].at[tail], full))

    def tail(self, core, i, k):
        return piece(self.kinds[i], core, k, self.shards[i].shape[-1])

    def part(self, i, tail, box):
        return self.fulls[i].at[box + tail]

    def number(self, core, i, k, e):
        return ((core * len(self.kinds) + i) * 3 + k) * EVENTS + e

    def pass_on(self, core, i, k, full, e, box):
        self.sides[core].go(self.number(core, i, k, e), full(box), full(box), self.place.sibling)

    def own(self):
        n = len(self.kinds)
        for i in range(n):
            src, dst = self.shards[i], self.fulls[i].at[self.place.box(())]
            pltpu.make_async_remote_copy(src_ref=src, dst_ref=dst, send_sem=self.keep.send.at[i],
                                         recv_sem=self.keep.send.at[n + i], device_id=self.place.sibling,
                                         device_id_type=MESH).start()

    def own_landed(self):
        n = len(self.kinds)
        for i in range(n):
            src, dst = self.shards[i], self.fulls[i].at[self.place.box(())]
            pltpu.make_async_remote_copy(src_ref=src, dst_ref=dst, send_sem=self.keep.send.at[i],
                                         recv_sem=self.keep.send.at[n + i], device_id=self.place.sibling,
                                         device_id_type=MESH).wait()

    def step(self, *arrays):
        def one(core):
            for i in arrays:
                for u in self.units[core][i]:
                    next(u, None)

        self.place.on_core(one)

    def whole(self, *arrays):
        def one(core):
            other = 1 - core
            for i in arrays:
                for k in range(3):
                    tail = self.tail(other, i, k)
                    if tail is None:
                        continue
                    for e, box in enumerate(passed_on(self.place, other, ORDERS[other][k])):
                        self.sides[other].landed(self.number(other, i, k, e), self.part(i, tail, box),
                                                 self.place.sibling)

        self.place.on_core(one)

    def end(self):
        def one(core):
            self.wires[core].sent()
            self.sides[core].sent()

        self.place.on_core(one)


def dot(a, b, dims=((1,), (0,))):
    return lax.dot_general(a, b, (dims, ((), ())), preferred_element_type=F32)


def exact(a, b, dims=((1,), (0,))):
    return lax.dot_general(a, b, (dims, ((), ())), precision=lax.Precision.HIGHEST, preferred_element_type=F32)


def iota(shape, dim):
    return lax.broadcasted_iota(jnp.int32, shape, dim)


def over24(i):
    return (i * 2731) >> 16


def ones_where(hit):
    return jnp.where(hit, 1.0, 0.0).astype(BF)


def picks():
    i, j = iota((768, 1024), 0), iota((768, 1024), 1)
    proj = ones_where(j == i + 8 * over24(i))
    i, j = iota((128, 1024), 0), iota((128, 1024), 1)
    at = 32 * (i >> 2) + (i & 3)
    hid, cls = ones_where(j == at + 24), ones_where(j == at + 28)
    i, j = iota((32, 1024), 0), iota((32, 1024), 1)
    misc = ones_where(j == 32 * i + 28)
    return proj, hid, cls, misc


def spread(first, size, per):
    i, l = iota((128, size), 0), iota((128, size), 1)
    block = over24(l) if per == 24 else l >> 2
    w, m = iota((32, size), 0), iota((32, size), 1)
    held = over24(m) if per == 24 else m >> 2
    return ones_where(i - first == l - per * block), held == w


ROWS = (("gain_attn", 16, 768, 24), ("gain_ffn", 40, 768, 24), ("pool", 64, 128, 4))


def normalise(h):
    centre = h - jnp.mean(h, axis=-1, keepdims=True)
    r = lax.rsqrt(jnp.mean(centre * centre, axis=-1, keepdims=True) + 1e-06)
    return centre * r, r


def norm_back(g, gain, n, r):
    gn = g * gain
    return r * (gn - jnp.mean(gn, axis=-1, keepdims=True) - n * jnp.mean(gn * n, axis=-1, keepdims=True))


TANH_A = 0.7978845608028654
TANH_B = 0.7978845608028654 * 0.044715


def gelu(u):
    u2 = u * u
    h = 0.5 + 0.5 * jnp.tanh(u * (TANH_A + TANH_B * u2))
    y = u * h
    return y, h + y * (1.0 - h) * (2.0 * TANH_A + 6.0 * TANH_B * u2)


def at_block(i):
    return i // 8, (i // 2) % 4, i % 2


def join(blocks, whole):
    def one(i, carry):
        x, z, y = at_block(i)
        pair = jnp.concatenate([blocks[x, z, 2 * y], blocks[x, z, 2 * y + 1]], axis=0)
        whole[pl.ds(pl.multiple_of(i * 48, 48), 48), :] = pair
        return carry

    lax.fori_loop(0, 16, one, 0)


def loop(n, step):
    def one(i, carry):
        step(i)
        return carry

    lax.fori_loop(0, n, one, 0)


def span(i, size):
    return pl.ds(pl.multiple_of(i * size, size), size)


def halves():
    lane = iota((1, 128), 1)
    return jnp.where(lane < 64, 1.0, 0.0), jnp.where(lane < 64, 0.0, 1.0)


KINDS = ("small", "cols", "cols", "cols", "cols")
SMALL, QKV, OUT, UP, DOWN = range(5)


def forward_kernel(tokens, cot, alive, alive_seq, cotl, s_small, s_qkv, s_out, s_up, s_down,
                   o_act, o_logits, o_wqkv, o_wout, o_wup, o_wdown, o_merged, o_probs, o_ctx, o_normed, o_n1, o_r1,
                   o_active, o_dact, o_gsec, o_dlow, o_tokens2, o_small, rows,
                   b_small, b_qkv, b_out, b_up, b_down, w_qkv, w_out, w_up, tok, cotv, merged, probs, ctx, normed, n1, r1,
                   active, dact, gsec, r2, dlow, out, projected, gproj, wproj, hid, cls,
                   send, recv, ssend, srecv, lsem, insem, outsem, xsend, xrecv):
    place = Place()
    loads = [pltpu.make_async_copy(tokens, tok, insem.at[0]), pltpu.make_async_copy(cot, cotv, insem.at[1])]
    for c in loads:
        c.start()
    greet(place)
    g = Gather(place, KINDS, (s_small, s_qkv, s_out, s_up, s_down), (b_small, b_qkv, b_out, b_up, b_down),
               send, recv, ssend, srecv, lsem)
    stores = []
    cross = Wire(xsend, xrecv)

    def keep(src, dst):
        c = pltpu.make_async_copy(src, dst, outsem.at[len(stores)])
        c.start()
        stores.append(c)

    def share(n, src, dst):
        keep(src, dst.at[0])
        cross.go(n, src, dst.at[1], place.sibling)

    g.step(QKV, OUT, SMALL, UP, DOWN)
    g.own()
    loads[0].wait()
    share(0, tok, o_tokens2)
    g.own_landed()
    g.step(QKV, OUT, SMALL, UP, DOWN)
    g.step(QKV, OUT, SMALL, UP, DOWN)
    g.step(QKV, OUT, SMALL)
    g.step(QKV, OUT, SMALL)
    g.step(UP, DOWN)
    g.step(QKV, SMALL)
    g.step(UP, DOWN)
    g.whole(QKV, SMALL)
    join(b_qkv, w_qkv)

    def qkv(j):
        c = span(j, 384)
        merged[:, c] = dot(tok[...], w_qkv[:, c]).astype(BF)

    loop(6, qkv)
    keep(w_qkv, o_wqkv)
    keep(merged, o_merged)

    p_proj, p_hid, p_cls, p_misc = picks()
    pack = b_small[...].reshape(1024, 128)
    wproj[...] = dot(p_proj, pack).astype(BF)
    hid[...] = dot(p_hid, pack)
    cls[...] = jnp.where(iota((128, 128), 1) < 14, dot(p_cls, pack), 0.0)
    misc = dot(p_misc, pack).astype(BF)
    for n, (name, first, size, per) in enumerate(ROWS):
        tile, held = spread(first, size, per)
        row = jnp.sum(jnp.where(held, dot(misc, tile), 0.0), axis=0, keepdims=True)
        rows[n, :, pl.ds(0, size)] = jnp.broadcast_to(row, (8, size))
    low_half, high_half = halves()
    g.step(OUT)

    qa, qb = (low_half * 0.125).astype(BF), (high_half * 0.125).astype(BF)

    def attend(s):
        r = span(s, SEQ)
        for p in range(PAIRS):
            q, k, v = (merged[r, pl.ds(768 * a + 128 * p, 128)] for a in range(3))
            scores = dot(jnp.concatenate([q * qa, q * qb], axis=0), k, ((1,), (1,)))
            e = jnp.exp(scores - jnp.max(scores, axis=-1, keepdims=True))
            pr = (e * (1.0 / jnp.sum(e, axis=-1, keepdims=True))).astype(BF)
            probs[s * PAIRS + p] = pr
            both = dot(pr, v)
            ctx[r, pl.ds(128 * p, 128)] = (both[:SEQ] * low_half + both[SEQ:] * high_half).astype(BF)

    loop(SEQ_DEV, attend)
    keep(probs, o_probs)
    share(1, ctx, o_ctx)
    g.whole(OUT)
    join(b_out, w_out)
    gain1 = rows[0, pl.ds(0, 1), :]

    def mix(j):
        r = span(j, 384)
        n, inv = normalise(tok[r, :].astype(F32) + dot(ctx[r, :], w_out[...]))
        n1[r, :] = n.astype(BF)
        normed[r, :] = (n * gain1).astype(BF)
        r1[r, :] = jnp.broadcast_to(inv, (384, 128))

    loop(2, mix)
    keep(w_out, o_wout)
    keep(n1, o_n1)
    keep(r1, o_r1)
    share(2, normed, o_normed)
    g.step(UP)
    g.whole(UP)
    join(b_up, w_up)

    def upward(j):
        c = span(j, 512)
        y, dy = gelu(dot(normed[...], w_up[:, c]))
        active[:, c] = y.astype(BF)
        dact[:, c] = dy.astype(BF)

    loop(6, upward)
    share(3, active, o_active)
    keep(dact, o_dact)
    keep(w_up, o_wup)
    g.step(DOWN)
    g.whole(DOWN)
    keep(b_down, o_wdown)
    loads[1].wait()
    gain2 = rows[1, pl.ds(0, 1), :]

    def downward(j):
        r = span(j, 384)
        second = normed[r, :].astype(F32) + dot(active[r, :], b_down[...].reshape(FF, D))
        n, inv = normalise(second)
        gsec[r, :] = n
        r2[r, :] = jnp.broadcast_to(inv, (384, 128))
        low = (n * gain2).astype(BF)
        out[r, :] = low
        projected[r, :] = dot(low, wproj[...])

    loop(2, downward)

    query = rows[2, pl.ds(0, 1), pl.ds(0, 128)]
    whole = low_half + high_half
    weights, pooled = [], []
    for s in range(SEQ_DEV):
        pr = projected[pl.ds(s * SEQ, SEQ), :]
        t = pr * query
        per_head = []
        for half in (low_half, high_half):
            score = jnp.sum(t * half, axis=-1, keepdims=True) * 0.125
            e = jnp.exp(score - jnp.max(score, axis=0, keepdims=True))
            per_head.append(e / jnp.sum(e, axis=0, keepdims=True))
        weights.append(per_head)
        pooled.append(jnp.sum(pr * (per_head[0] * low_half + per_head[1] * high_half), axis=0, keepdims=True))
    none = jnp.zeros((1, 128), F32)
    pooled = jnp.concatenate(pooled + [none, none], axis=0)
    hidden = jnp.tanh(exact(pooled, hid[...]))
    o_logits[...] = exact(hidden, cls[...]) * alive_seq[...]
    g_log = cotl[...] * alive_seq[...]
    o_small[1] = exact(hidden, g_log, ((0,), (0,))).astype(BF)
    g_pre = exact(g_log, cls[...], ((1,), (1,))) * (1.0 - hidden * hidden)
    o_small[0] = exact(pooled, g_pre, ((0,), (0,))).astype(BF)
    g_pooled = exact(g_pre, hid[...], ((1,), (1,)))
    g_query = none
    for s in range(SEQ_DEV):
        r = pl.ds(s * SEQ, SEQ)
        pr = projected[r, :]
        gp = g_pooled[s:s + 1]
        t = pr * gp
        total = (weights[s][0] * low_half + weights[s][1] * high_half) * gp
        for half, w in zip((low_half, high_half), weights[s]):
            dw = jnp.sum(t * half, axis=-1, keepdims=True)
            ds = w * (dw - jnp.sum(w * dw, axis=0, keepdims=True)) * 0.125
            total = total + ds * (query * half)
            g_query = g_query + jnp.sum(ds * pr, axis=0, keepdims=True) * half
        gproj[r, :] = total.astype(BF)
    o_small[2] = jnp.broadcast_to(g_query, (128, 128)).astype(BF)

    def back(j):
        r = span(j, 384)
        keep_tok = alive[r, pl.ds(0, 1)]
        low = out[r, :]
        g_out = keep_tok * cotv[r, :].astype(F32) + dot(gproj[r, :], wproj[...], ((1,), (1,)))
        n = gsec[r, :]
        part = jnp.sum(g_out * n, axis=0, keepdims=True)
        rows[3, pl.ds(0, 1), :] = jnp.where(j == 0, part, part + rows[3, pl.ds(0, 1), :])
        g2 = norm_back(g_out, gain2, n, r2[r, pl.ds(0, 1)])
        gsec[r, :] = g2
        dlow[r, :] = g2.astype(BF)
        cotv[r, :] = (keep_tok * low.astype(F32)).astype(BF)

    loop(2, back)
    share(4, dlow, o_dlow)
    keep(gsec, o_gsec)
    keep(cotv, o_act)
    o_small[3:9] = dot(out[...], gproj[...], ((0,), (0,))).astype(BF).reshape(6, 128, 128)
    g.end()
    for c in stores:
        c.wait()
    for n, src, dst in ((0, tok, o_tokens2), (1, ctx, o_ctx), (2, normed, o_normed), (3, active, o_active), (4, dlow, o_dlow)):
        cross.landed(n, dst.at[1], place.sibling)
    cross.sent()


def forward(tokens, cot, alive, alive_seq, cotl, shards):
    hbm, vmem = pl.BlockSpec(memory_space=pl.ANY), pl.BlockSpec(memory_space=pltpu.VMEM)
    n = len(KINDS)
    count = n * 3 * EVENTS

    def arr(*shape, dtype=BF):
        return jax.ShapeDtypeStruct(shape, dtype)

    outs = [
        (arr(TOK, D), hbm), (arr(8, 128, dtype=F32), vmem),
        (arr(D, 3 * D), hbm), (arr(D, D), hbm), (arr(D, FF), hbm), (arr(2, 4, 4, 96, D), hbm),
        (arr(TOK, 3 * D), hbm), (arr(SEQ_DEV * PAIRS, 256, 128), hbm), (arr(2, TOK, D), hbm), (arr(2, TOK, D), hbm),
        (arr(TOK, D), hbm), (arr(TOK, 128, dtype=F32), hbm), (arr(2, TOK, FF), hbm), (arr(TOK, FF), hbm),
        (arr(TOK, D, dtype=F32), hbm), (arr(2, TOK, D), hbm), (arr(2, TOK, D), hbm),
        (arr(9, 128, 128), vmem), (arr(4, 8, D, dtype=F32), vmem),
    ]
    dma = pltpu.SemaphoreType.DMA
    scratch = [
        pltpu.VMEM((2, 4, 4, 32, 128), BF), pltpu.VMEM((2, 4, 4, 24, 3 * D), BF), pltpu.VMEM((2, 4, 4, 24, D), BF),
        pltpu.VMEM((2, 4, 4, 24, FF), BF), pltpu.VMEM((2, 4, 4, 96, D), BF),
        pltpu.VMEM((D, 3 * D), BF), pltpu.VMEM((D, D), BF), pltpu.VMEM((D, FF), BF),
        pltpu.VMEM((TOK, D), BF), pltpu.VMEM((TOK, D), BF), pltpu.VMEM((TOK, 3 * D), BF),
        pltpu.VMEM((SEQ_DEV * PAIRS, 256, 128), BF), pltpu.VMEM((TOK, D), BF), pltpu.VMEM((TOK, D), BF),
        pltpu.VMEM((TOK, D), BF), pltpu.VMEM((TOK, 128), F32), pltpu.VMEM((TOK, FF), BF), pltpu.VMEM((TOK, FF), BF),
        pltpu.VMEM((TOK, D), F32), pltpu.VMEM((TOK, 128), F32), pltpu.VMEM((TOK, D), BF), pltpu.VMEM((TOK, D), BF),
        pltpu.VMEM((TOK, 128), F32), pltpu.VMEM((TOK, 128), BF), pltpu.VMEM((D, 128), BF),
        pltpu.VMEM((128, 128), F32), pltpu.VMEM((128, 128), F32),
        dma((count,)), dma((count,)), dma((2 * count,)), dma((2 * count,)), dma((2 * n,)),
        dma((2,)), dma((20,)), dma((5,)), dma((5,)),
    ]
    return pl.pallas_call(
        forward_kernel,
        out_shape=[o for o, _ in outs],
        in_specs=[hbm, hbm, vmem, vmem, vmem] + [hbm] * n,
        out_specs=[s for _, s in outs],
        scratch_shapes=scratch,
        compiler_params=pltpu.CompilerParams(collective_id=0, has_side_effects=True, vmem_limit_bytes=VMEM),
        cost_estimate=pl.CostEstimate(flops=12 * 10**9, bytes_accessed=60 * 10**6, transcendentals=4 * 10**6),
        name="forward",
    )(tokens, cot, alive, alive_seq, cotl, *shards)


def landing(order):
    out, left = [], ["x", "z", "y"]
    for axis in reversed(order):
        left = [a for a in left if a != axis]
        out.append((1 if axis == "x" else 3, tuple(SIZE[a] for a in left)))
    return out


def add_box(place, held, left, fixed, terms):
    dims = tuple(SIZE[a] for a in left)

    def step(i):
        index = []
        for d in reversed(dims):
            index.append(i % d)
            i = i // d
        index = tuple(reversed(index))
        at = dict(zip(left, index))
        b = tuple(fixed[a] if a in fixed else at[a] if a in at else place.at(a) for a in ("x", "z", "y"))
        total = held[b]
        for t in terms:
            total = total + t[index]
        held[b] = total

    if dims:
        count = 1
        for d in dims:
            count *= d
        loop(count, step)
    else:
        step(0)


def reduce_unit(place, wire, side, base, base2, core, order, held, lands, last, result, twin, put):
    way = 1 if core == 0 else -1
    left, e = ["x", "z", "y"], base
    for axis, bufs in zip(reversed(order), lands):
        left = [a for a in left if a != axis]
        ahead, back = place.near(axis, way), place.near(axis, -way)
        mine = {axis: place.at(axis)}
        if axis == "x":
            wire.go(e, held.at[place.box(left, x=place.at("x", 1))], bufs[0], ahead)
            yield
            wire.landed(e, bufs[0], ahead)
            add_box(place, held, left, mine, [bufs[0]])
            e += 1
        else:
            wire.go(e, held.at[place.box(left, **{axis: place.at(axis, 2)})], bufs[0], ahead)
            wire.go(e + 1, held.at[place.box(left, **{axis: place.at(axis, -way)})], bufs[1], back)
            yield
            wire.landed(e, bufs[0], ahead)
            onward = {axis: place.at(axis, way)}
            add_box(place, held, left, onward, [bufs[0]])
            wire.go(e + 2, held.at[place.box(left, **onward)], bufs[2], ahead)
            yield
            wire.landed(e + 1, bufs[1], ahead)
            wire.landed(e + 2, bufs[2], ahead)
            add_box(place, held, left, mine, [bufs[1], bufs[2]])
            e += 3
    own = place.box(())
    wire.go(e, held.at[own], last, place.near("x", 2))
    yield
    wire.landed(e, last, place.near("x", 2))
    total = held[own] + last[...]
    result[...] = total
    side.go(base2, result, twin, place.sibling)
    put[0][...] = total.astype(F32)
    yield
    side.landed(base2, twin, place.sibling)
    put[1][...] = twin[...].astype(F32)


STEPS = 8
PIECES = [(i, k) for i in (DOWN, UP, OUT, QKV, SMALL) for k in range(3) if i != SMALL or k == 1]


def piece_shape(i):
    return {SMALL: (16, 128), QKV: (24, 384), OUT: (24, 128), UP: (24, 512), DOWN: (96, 128)}[i]


def reduce_scratch():
    out = []
    for i, k in PIECES:
        shape = piece_shape(i)
        out.append(pltpu.VMEM((2, 4, 4) + shape, BF))
        for copies, dims in landing(ORDERS[0][k]):
            out.extend([pltpu.VMEM(dims + shape, BF)] * copies)
        out.extend([pltpu.VMEM(shape, BF)] * 3)
    return out


class Reduce:
    def __init__(self, place, scratch, outs, send, recv, ssend, srecv):
        self.place = place
        self.wires = [Wire(send, recv) for _ in range(2)]
        self.sides = [Wire(ssend, srecv) for _ in range(2)]
        self.held, self.units, self.live, self.done = {}, [{}, {}], [], {}
        for n, (i, k) in enumerate(PIECES):
            held = scratch.pop(0)
            lands = [[scratch.pop(0) for _ in range(copies)] for copies, _ in landing(ORDERS[0][k])]
            last, result, twin = (scratch.pop(0) for _ in range(3))
            self.held[i, k] = held
            for core in range(2):
                kind = "small" if i == SMALL else "cols"
                width = outs[i].shape[-1]
                put = (outs[i].at[piece(kind, core, k, width)], outs[i].at[piece(kind, 1 - core, k, width)])
                self.units[core][i, k] = reduce_unit(
                    place, self.wires[core], self.sides[core], n * SUMS, n, core, ORDERS[core][k],
                    held, lands, last, result, twin, put)

    def advance(self, pieces):
        def one(core):
            for p in pieces:
                next(self.units[core][p], None)

        self.place.on_core(one)

    def start(self, *pieces):
        self.advance(pieces)
        for p in pieces:
            self.live.append(p)
            self.done[p] = 1

    def pump(self, *arrays):
        todo = [p for p in self.live if not arrays or p[0] in arrays]
        self.advance(todo)
        for p in todo:
            self.done[p] += 1
            if self.done[p] == STEPS:
                self.live.remove(p)

    def end(self):
        while self.live:
            self.pump()

        def one(core):
            self.wires[core].sent()
            self.sides[core].sent()

        self.place.on_core(one)


def lay(held, value):
    for i in range(16):
        x, z, y = at_block(i)
        for j in range(2):
            held[x, z, 2 * y + j] = value[48 * i + 24 * j:48 * i + 24 * j + 24].astype(BF)


def backward_kernel(tokens2, merged_h, probs_h, ctx2_h, normed2_h, n1_h, r1_h, active2_h, dact_h, gsec_h, dlow2_h,
                    wqkv_h, wout_h, wup_h, wdown_h, small, rows,
                    o_gtok, o_qkv, o_out, o_up, o_down, o_small,
                    tok2, act2, dact, normed2, ctx2, dlow2, n1, r1, gsec, attn, attn_s, gctx, gup_s, gm_s, probs,
                    w_big, w_small, w_out, packed, packed_s, *rest):
    scratch = list(rest[:-8])
    send, recv, ssend, srecv, insem, wsem, xsend, xrecv = rest[-8:]
    place = Place()
    core = place.core
    loads = {}

    def load(name, src, dst):
        c = pltpu.make_async_copy(src, dst, insem.at[len(loads)])
        c.start()
        loads[name] = c

    def ready(*names):
        for name in names:
            loads[name].wait()

    def w_load(i, src, dst):
        c = pltpu.make_async_copy(src, dst, wsem.at[i])
        return c

    load("dlow", dlow2_h, dlow2)
    for j in range(2):
        w_load(j, wdown_h.at[0, j], w_small.at[j]).start()
    load("dact", dact_h, dact)
    load("active", active2_h, act2)
    load("normed", normed2_h, normed2)
    load("gsec", gsec_h, gsec)
    load("n1", n1_h, n1)
    load("r1", r1_h, r1)
    load("wout", wout_h, w_out)
    load("ctx", ctx2_h, ctx2)
    load("probs", probs_h, probs)
    load("tokens", tokens2, tok2)
    greet(place)
    red = Reduce(place, scratch, {QKV: o_qkv, OUT: o_out, UP: o_up, DOWN: o_down, SMALL: o_small},
                 send, recv, ssend, srecv)
    cross = Wire(xsend, xrecv)

    def mine(size):
        return pl.ds(pl.multiple_of(core * size, 128), size)

    def other(size):
        return pl.ds(pl.multiple_of((1 - core) * size, 128), size)

    ready("dlow", "dact")
    for j in range(8):
        slot = j % 2
        w_load(slot, wdown_h.at[j // 4, j % 4], w_small.at[slot]).wait()
        c = pl.ds(384 * j, 384)
        g = dot(dlow2[0], w_small[slot].reshape(384, D), ((1,), (1,)))
        dact[:, c] = (g * dact[:, c].astype(F32)).astype(BF)
        if j + 2 < 8:
            w_load(slot, wdown_h.at[(j + 2) // 4, (j + 2) % 4], w_small.at[slot]).start()
    gup = dact
    cross.go(0, gup.at[:, other(FF // 2)], gup_s, place.sibling)
    for j in range(2):
        w_load(2 + j, wup_h.at[pl.ds(256 * j, 256)], w_big.at[j]).start()
    ready("active")

    def down(j):
        r = span(j, 384)
        right = dlow2[:, :, mine(384)].reshape(2 * TOK, 384)
        g = dot(act2[:, :, r].reshape(2 * TOK, 384), right, ((0,), (0,))).astype(BF)
        for k in range(3):
            red.held[DOWN, k][j // 4, j % 4] = g[:, 128 * k:128 * k + 128].reshape(4, 96, 128)

    loop(8, down)
    red.start((DOWN, 0), (DOWN, 1), (DOWN, 2))
    ready("normed")
    load("merged", merged_h, act2.at[0, :, pl.ds(0, 3 * D)])
    merged = act2.at[0, :, pl.ds(0, 3 * D)]
    cross.landed(0, gup_s, place.sibling)
    for k in range(3):
        own = gup[:, pl.ds(pl.multiple_of(core * (FF // 2) + 512 * k, 128), 512)]
        lay(red.held[UP, k], dot(normed2[0], own, ((0,), (0,))) + dot(normed2[1], gup_s[:, 512 * k:512 * k + 512], ((0,), (0,))))
        red.start((UP, k))
        if k == 1:
            red.pump(DOWN)
    ready("gsec", "n1", "r1")
    for j in range(3):
        slot = j % 2
        w_load(2 + slot, wup_h.at[pl.ds(256 * j, 256)], w_big.at[slot]).wait()
        c = pl.ds(256 * j, 256)
        gsec[:, c] = gsec[:, c] + dot(gup[...], w_big[slot], ((1,), (1,)))
        if j == 0:
            w_load(2, wup_h.at[pl.ds(512, 256)], w_big.at[0]).start()
        red.pump(*((DOWN,) if j == 0 else ()))
    for j in range(2):
        w_load(2 + (j + 1) % 2, wqkv_h.at[pl.ds(256 * j, 256)], w_big.at[(j + 1) % 2, :, pl.ds(0, 3 * D)]).start()
    gain1 = rows[0, pl.ds(0, 1), :]

    def norm1(j, total):
        r = span(j, 384)
        g, n = gsec[r, :], n1[r, :].astype(F32)
        total = total + jnp.sum(g * n, axis=0, keepdims=True)
        g = norm_back(g, gain1, n, r1[r, pl.ds(0, 1)])
        gsec[r, :] = g
        attn[r, :] = g.astype(BF)
        return total

    g_gain1 = lax.fori_loop(0, 2, norm1, jnp.zeros((1, D), F32))
    cross.go(1, attn.at[:, other(384)], attn_s, place.sibling)
    ready("wout", "ctx")

    def context(j):
        r = span(j, 384)
        gctx[r, :] = dot(attn[r, :], w_out[...], ((1,), (1,))).astype(BF)

    loop(2, context)
    red.pump()

    p_proj, p_hid, p_cls, p_misc = picks()
    pack = dot(p_proj, small[3:9].reshape(D, 128), ((0,), (0,)))
    pack = pack + dot(p_hid, small[0], ((0,), (0,)))
    lane = iota((128, 128), 1)
    pack = pack + dot(p_cls, jnp.where(lane < 14, small[1].astype(F32), 0.0).astype(BF), ((0,), (0,)))
    values = (g_gain1, rows[3, pl.ds(0, 1), :], small[2, pl.ds(0, 1), :].astype(F32))
    misc = jnp.zeros((32, 128), F32)
    for (name, first, size, per), value in zip(ROWS, values):
        tile, held = spread(first, size, per)
        misc = misc + dot(jnp.where(held, value, 0.0).astype(BF), tile, ((1,), (1,)))
    packed[...] = (pack + dot(p_misc, misc.astype(BF), ((0,), (0,)))).astype(BF).reshape(2, 4, 4, 32, 128)
    place.on_core(lambda c: cross.copy(3, packed.at[:, :, :, pl.ds(16 - 16 * c, 16)], packed_s, place.sibling).start())

    cross.landed(1, attn_s, place.sibling)
    g = dot(ctx2[0], attn[:, mine(384)], ((0,), (0,))) + dot(ctx2[1], attn_s[...], ((0,), (0,)))
    for k in range(3):
        lay(red.held[OUT, k], g[:, 128 * k:128 * k + 128])
    cross.landed(3, packed_s, place.sibling)

    def small_half(c):
        red.held[SMALL, 1][...] = packed[:, :, :, 16 * c:16 * c + 16, :] + packed_s[...]

    place.on_core(small_half)
    red.start((OUT, 0), (OUT, 1), (OUT, 2), (SMALL, 1))
    ready("merged", "probs")

    low_half, high_half = halves()
    la, lb = low_half.astype(BF), high_half.astype(BF)
    qa, qb = (low_half * 0.125).astype(BF), (high_half * 0.125).astype(BF)

    def attend_back(s):
        r = span(s, SEQ)
        for p in range(PAIRS):
            at = [pl.ds(768 * a + 128 * p, 128) for a in range(3)]
            q, k, v = (merged[r, c] for c in at)
            d = gctx[r, pl.ds(128 * p, 128)]
            d2 = jnp.concatenate([d * la, d * lb], axis=0)
            q2 = jnp.concatenate([q * qa, q * qb], axis=0)
            pr = probs[s * PAIRS + p]
            gp = dot(d2, v, ((1,), (1,)))
            merged[r, at[2]] = dot(pr, d2, ((0,), (0,))).astype(BF)
            pf = pr.astype(F32)
            t = pf * gp
            gs = (t - pf * jnp.sum(t, axis=-1, keepdims=True)).astype(BF)
            both = dot(gs, k)
            merged[r, at[0]] = ((both[:SEQ] * low_half + both[SEQ:] * high_half) * 0.125).astype(BF)
            merged[r, at[1]] = dot(gs, q2, ((0,), (0,))).astype(BF)

    for part in range(3):
        lax.fori_loop(2 * part, 2 * part + 2, lambda s, c: (attend_back(s), c)[1], 0)
        red.pump()
    cross.go(2, act2.at[0, :, other(3 * D // 2)], gm_s, place.sibling)
    ready("tokens")

    def tokens_part(j):
        slot = (j + 1) % 2
        w_load(2 + slot, wqkv_h.at[pl.ds(256 * j, 256)], w_big.at[slot, :, pl.ds(0, 3 * D)]).wait()
        c = pl.ds(256 * j, 256)
        gsec[:, c] = gsec[:, c] + dot(merged[...], w_big[slot, :, :3 * D], ((1,), (1,)))

    tokens_part(0)
    w_load(3, wqkv_h.at[pl.ds(512, 256)], w_big.at[1, :, pl.ds(0, 3 * D)]).start()
    red.pump()
    cross.landed(2, gm_s, place.sibling)
    for k in range(3):
        own = merged[:, pl.ds(pl.multiple_of(core * (3 * D // 2) + 384 * k, 128), 384)]
        lay(red.held[QKV, k], dot(tok2[0], own, ((0,), (0,))) + dot(tok2[1], gm_s[:, 384 * k:384 * k + 384], ((0,), (0,))))
        red.start((QKV, k))
    red.pump()
    tokens_part(1)
    red.pump()
    tokens_part(2)
    store = pltpu.make_async_copy(gsec, o_gtok, insem.at[len(loads)])
    store.start()
    red.end()
    cross.sent()
    place.on_core(lambda c: cross.copy(3, packed.at[:, :, :, pl.ds(16 - 16 * c, 16)], packed_s, place.sibling).wait_send())
    store.wait()


def backward(*args):
    hbm, vmem = pl.BlockSpec(memory_space=pl.ANY), pl.BlockSpec(memory_space=pltpu.VMEM)

    def arr(*shape, dtype=F32):
        return jax.ShapeDtypeStruct(shape, dtype)

    dma = pltpu.SemaphoreType.DMA
    count = len(PIECES)
    scratch = [
        pltpu.VMEM((2, TOK, D), BF), pltpu.VMEM((2, TOK, FF), BF), pltpu.VMEM((TOK, FF), BF),
        pltpu.VMEM((2, TOK, D), BF), pltpu.VMEM((2, TOK, D), BF), pltpu.VMEM((2, TOK, D), BF),
        pltpu.VMEM((TOK, D), BF), pltpu.VMEM((TOK, 128), F32), pltpu.VMEM((TOK, D), F32),
        pltpu.VMEM((TOK, D), BF), pltpu.VMEM((TOK, D // 2), BF), pltpu.VMEM((TOK, D), BF),
        pltpu.VMEM((TOK, FF // 2), BF), pltpu.VMEM((TOK, 3 * D // 2), BF),
        pltpu.VMEM((SEQ_DEV * PAIRS, 256, 128), BF),
        pltpu.VMEM((2, 256, FF), BF), pltpu.VMEM((2, 4, 96, D), BF), pltpu.VMEM((D, D), BF),
        pltpu.VMEM((2, 4, 4, 32, 128), BF), pltpu.VMEM((2, 4, 4, 16, 128), BF),
    ] + reduce_scratch() + [
        dma((count * SUMS,)), dma((count * SUMS,)), dma((count,)), dma((count,)), dma((16,)), dma((4,)), dma((4,)), dma((4,)),
    ]
    return pl.pallas_call(
        backward_kernel,
        out_shape=[arr(TOK, D), arr(24, 3 * D), arr(24, D), arr(24, FF), arr(96, D), arr(32, 128)],
        in_specs=[hbm] * 15 + [vmem] * 2,
        out_specs=[hbm] + [vmem] * 5,
        scratch_shapes=scratch,
        compiler_params=pltpu.CompilerParams(collective_id=1, has_side_effects=True, vmem_limit_bytes=VMEM),
        cost_estimate=pl.CostEstimate(flops=24 * 10**9, bytes_accessed=60 * 10**6, transcendentals=0),
        name="backward",
    )(*args)


def local(tokens, exit_layer, w_qkv, w_out, gain_attn, w_up, w_down, gain_ffn, w_proj, pool_query, w_hid, w_cls,
          cot_out, cot_logits):
    line = jnp.concatenate([gain_attn, gain_ffn, pool_query])
    last = jnp.pad(w_cls, ((0, 0), (0, 128 - 14)))
    last = last + jnp.pad(line[None], ((0, 3), (16, 128 - 16 - line.shape[0])))
    small = jnp.concatenate([w_proj, w_hid, last], axis=0)
    alive = (exit_layer >= LAYER).astype(F32)
    alive_tok = jnp.broadcast_to(jnp.repeat(alive, SEQ)[:, None], (TOK, 128))
    alive_seq = jnp.broadcast_to(jnp.pad(alive, (0, 2))[:, None], (8, 128))
    cotl = jnp.pad(cot_logits, ((0, 2), (0, 128 - 14)))
    (act, logits, f_qkv, f_out, f_up, f_down, merged, probs, ctx, normed, n1, r1, active, dact, gsec, dlow, tokens2,
     small_g, rows) = forward(tokens, cot_out, alive_tok, alive_seq, cotl, (small, w_qkv, w_out, w_up, w_down))
    g_tok, g_qkv, g_out, g_up, g_down, g_small = backward(
        tokens2, merged, probs, ctx, normed, n1, r1, active, dact, gsec, dlow, f_qkv, f_out, f_up, f_down, small_g, rows)
    line = g_small[28]
    return (act, logits[:SEQ_DEV, :14], g_tok, g_qkv, g_out, line[16:40], g_up, g_down, line[40:64],
            g_small[:24], line[64:68], g_small[24:28], g_small[28:32, :14])


def solution(mesh):
    both, wide = P(("wide", "grp"), None), P("wide", None)
    in_specs = (both, P(("wide", "grp")), wide, wide, P("wide"), wide, wide, P("wide"), wide, P("wide"), wide, wide,
                both, both)
    out_specs = (both, both, both, wide, wide, P("wide"), wide, wide, P("wide"), wide, P("wide"), wide, wide)
    return jax.shard_map(local, mesh=mesh, in_specs=in_specs, out_specs=out_specs, check_vma=False)
```

time: 915 us -> 217 us (0.24)
  waiting for transfers between devices: 360 us -> 0 us
  Pallas kernels: 0 us -> 194 us
  blocking collectives: 178 us -> 0 us
  local copies, waits for them, and re-layouts: 189 us -> 15.3 us
  matrix products: 108 us -> 0 us
  starting transfers between devices: 34.4 us -> 0 us
  other arithmetic: 20.7 us -> 3.49 us
  between operations: 14.9 us -> 0.98 us
    pallas_call x0 -> x2, Pallas kernels: none -> 194 us  [the longest x1 104 us: backward(): pl.pallas_call(backward_kernel, out_shape=[arr(TOK, D), arr(24, 3 * D), a...]
    reduce_scatter x1 -> x0, waiting for transfers between devices: 193 us -> none  [sum_together(): lax.psum_scatter(lines, axis, tiled=True).reshape(-1)]
    all_gather x2 -> x0, blocking collectives: 142 us -> none  [side_by_side(): out, at, outs = (lax.all_gather(both, axis, axis=dim, tiled=True), 0, [])]
    all_gather x2 -> x0, waiting for transfers between devices: 134 us -> none  [the longest x1 128 us: local(): lax.all_gather(w_down, 'wide', axis=0, tiled=True)]
    dot_general x31 -> x0, matrix products: 108 us -> none  [the longest x1 14 us: local(): jnp.einsum('nd,fd->nf', down_low, full_down, preferred_element_type=jnp.f...]
    unnamed x164 -> x21, local copies, waits for them, and re-layouts: 87.3 us -> 5.79 us
    all_to_all x2 -> x0, blocking collectives: 35.9 us -> none  [from_everyone(): lax.all_to_all(jnp.broadcast_to(shard[None], (peers, *shard.shape)), axis...]
    reshape x13 -> x0, local copies, waits for them, and re-layouts: 34.4 us -> none  [the longest x1 13.3 us: sum_together(): jnp.pad(lines, ((0, 0), (0, span * 128 - lines.shape[1]))).reshape(-1, 128)]
  transfers between devices with their start and end apart: 11 -> 0, of which waited for: 10 -> 0; matrix products, arithmetic and copies ran while one was open for 7% -> 0% of each run, Pallas kernels for 0% -> 0%
where the time goes in v1:
time: 217 us; the launch traced here: 214 us
  Pallas kernels  194 us (89%)
  local copies, waits for them, and re-layouts  15.3 us (7%)
  other arithmetic  3.49 us (2%)
    pallas_call x1, Pallas kernels, backward(): pl.pallas_call(backward_kernel, out_shape=[arr(TOK, D), arr(24, 3 * D), a...  104 us
    pallas_call x1, Pallas kernels, forward(): pl.pallas_call(forward_kernel, out_shape=[o for o, _ in outs], in_specs=[...  90.8 us
    unnamed x21, local copies, waits for them, and re-layouts  5.79 us

profile of v1, /device:TPU:1, one launch (start us, length us, event | category | flops | bytes accessed | tf_op | source)
XLA Modules:
  0.0 214.1 jit_solution(15240623736199568611)
XLA Ops:
  0.6 0.7 compare_convert_fusion
  1.3 0.8 maximum_bitcast_fusion
  2.1 0.8 pad_add_fusion
  2.8 0.1 broadcast_bitcast_fusion
  2.9 0.7 broadcast_in_dim.22.alive_seq
  3.6 1.3 pad.17.cotl
  4.8 1.3 pad_maximum_fusion.s_small
  6.2 0.9 broadcast_in_dim.21.alive
  7.1 90.8 %forward.1 = (bf16[768,768]{1,0:T(8,128)(2,1)}, f32[8,128]{1,0:T(8,128)}, bf16[768,2304]{1,0:T(8,128)(2,1)}, bf16[768,768]{1,0:T(8,128)(2,1)}, bf16[768,3072]{1,...) custom-call(bf16[768,768]{1,0:T(8,128)(2,1)} %tokens.1, ...), custom_call_target="tpu_custom_call" | custom-call | flops 12000000000 | bytes 60000000 | tf_op jit(solution)/shard_map/forward/pallas_call | solution.py:544
  97.9 0.0 copy-start.1
  97.9 103.5 %backward.1 = (f32[768,768]{1,0:T(8,128)}, f32[24,2304]{1,0:T(8,128)}, f32[24,768]{1,0:T(8,128)}, f32[24,3072]{1,0:T(8,128)}, f32[96,768]{1,0:T(8,128)}, /*index=5*/f32[32,128]{1,0:T(8,128)}) custom-call(bf16[2,768,768]{2,1,0:T(8,128)(2,1)} %get-tuple-element.40.tokens2, bf16[768,2304]{1,0:T(8,128)(2,1)} %get-tuple-element.41.merged_h, ...), custom_call_target="tpu_custom_call" | custom-call | flops 24000000000 | bytes 60000000 | tf_op jit(solution)/shard_map/backward/pallas_call | solution.py:920
  201.4 0.0 copy-start.6
  201.4 0.0 copy-start
  201.4 1.4 slice_bitcast_fusion
  202.8 1.3 slice_bitcast_fusion.1
  204.2 1.3 slice.42
  205.4 1.3 slice.43
  206.7 1.3 slice.39
  208.0 0.0 copy-done.1
  208.0 1.0 copy.34
  209.0 0.0 copy-done.6
  209.0 0.6 copy.35
  209.6 0.0 copy-done
  209.6 0.0 copy-start.4
  209.6 0.0 copy-start.5
  209.6 0.0 copy-start.3
  209.6 0.0 copy-start.2
  209.6 1.4 copy.36
  211.0 0.0 copy-done.4
  211.0 0.7 copy.37
  211.7 0.0 copy-done.5
  211.7 0.6 copy.38
  212.4 0.0 copy-done.3
  212.4 0.7 copy.39
  213.1 0.0 copy-done.2
  213.1 0.7 copy.40
  (1 shorter events, 0.0 us)
Async XLA Ops:
  97.9 110.1 %copy-start.1 = (bf16[768,768]{1,0:T(8,128)(2,1)S(1)}, bf16[768,768]{1,0:T(8,128)(2,1)}, u32[]{:S(2)}) copy-start(bf16[768,768]{1,0:T(8,128)(2,1)} %get-tuple-element.78) | copy-start | bytes 3538948
  201.4 7.6 %copy-start.6 = (f32[8,128]{1,0:T(8,128)S(1)}, f32[8,128]{1,0:T(8,128)}, u32[]{:S(2)}) copy-start(f32[8,128]{1,0:T(8,128)} %get-tuple-element.39) | copy-start | bytes 12292
  201.4 8.2 %copy-start = (f32[768,768]{1,0:T(8,128)S(1)}, f32[768,768]{1,0:T(8,128)}, u32[]{:S(2)}) copy-start(f32[768,768]{1,0:T(8,128)} %get-tuple-element.80) | copy-start | bytes 7077892
  209.6 1.4 copy-start.4
  209.6 2.1 copy-start.5
  209.6 2.7 %copy-start.3 = (f32[24,3072]{1,0:T(8,128)S(1)}, f32[24,3072]{1,0:T(8,128)}, u32[]{:S(2)}) copy-start(f32[24,3072]{1,0:T(8,128)} %get-tuple-element.84) | copy-start | bytes 884740
  209.6 3.5 %copy-start.2 = (f32[96,768]{1,0:T(8,128)S(1)}, f32[96,768]{1,0:T(8,128)}, u32[]{:S(2)}) copy-start(f32[96,768]{1,0:T(8,128)} %get-tuple-element.85) | copy-start | bytes 884740
